TPU v7x, 32 devices: a whole 2x2x4 slice. The times are simulated.
32 devices in a mesh: group: 2 (over y), tensor: 4 (over z), owner: 2 (over x), sub: 2 (over core).
Axes of the slice: x: 2, y: 2, z: 4, core: 2. Of those that a mesh axis runs over, the one named last changes fastest.
Arguments:
- activations: bfloat16 [3, 2048, 8192], P(None, 'group', 'tensor'), parts along dimension 1, may hold values from -6 to 6
- out_weight: bfloat16 [8192, 8192], P('tensor', ('owner', 'sub')), may hold values from -0.0625 to 0.0625
- shrink_base: bfloat16 [8192, 512], P('tensor'), may hold values from -0.0625 to 0.0625
- common_expand_matrix: bfloat16 [512, 8192], P('tensor', ('owner', 'sub')), may hold values from -0.25 to 0.25
- cores: bfloat16 [256, 512, 512], P(('owner', 'sub'), None, 'tensor'), may hold values from -0.25 to 0.25
- plan_ids: int32 [6, 4], P('group'), parts along dimension 0, may hold values from 0 to 255, as said below
- seg_slot: int32 [6, 8], P('group'), parts along dimension 0, may hold values from 0 to 3, as said below
- seg_length: int32 [6, 8], P('group'), parts along dimension 0, may hold values from 1 to 128, as said below
- owner_map: int32 [256], replicated, may hold values from 0 to 255, each once
Outputs:
- layer_out: bfloat16 [3, 2048, 8192], P(None, ('group', 'tensor'), ('owner', 'sub')), parts along dimension 1
There are 2 independent parts, one for each index of `group`. A program takes and returns all parts, laid end to end along the dimension named above; an argument that names none is the same for every part. Nothing has to cross between parts.
Inputs may be any that keep to these rules, and one draw needn't show every extreme that they name: `plan_ids`: the 4 adapters of each step are distinct. `seg_slot`: every entry of a step's plan is used by at least one segment of that step. `seg_length`: each step has a segment with all 128 rows live. `owner_map`: A permutation of the slots.
All inputs are finite; a program needn't handle non-finite values.
Results may differ from a plain program's by a relative error of at most 0.0043.
Values may be sent and summed in bfloat16 or wider, within the bound.
A program may use at most 192 MiB of HBM per device.

v0:
```python
import jax
import jax.numpy as jnp
from jax import lax
from jax.sharding import PartitionSpec as P

SEG = 128


def pick_cores(wanted, cores, owner_map):
    per_device = cores.shape[0]
    slots = owner_map[wanted]
    holder = slots // per_device
    local_index = slots % per_device
    chosen = cores[local_index].astype(jnp.float32)
    mine = holder == lax.axis_index(("owner", "sub"))
    return jnp.where(mine[:, None, None], chosen, jnp.float32(0.0))


def shards(
    activations,
    out_weight,
    shrink_base,
    common_expand_matrix,
    cores,
    plan_ids,
    seg_slot,
    seg_length,
    owner_map,
):
    step_count, row_count, feat_local = activations.shape
    segs_n = row_count // SEG
    rank_full = shrink_base.shape[1]
    rank_local = cores.shape[2]
    flattened = activations.reshape(step_count * row_count, feat_local)
    partial_value = jnp.dot(flattened, shrink_base, preferred_element_type=jnp.float32)
    shrunk = lax.psum(partial_value, "tensor").astype(jnp.bfloat16)
    shrunk = shrunk.reshape(step_count, segs_n, SEG, rank_full)
    step_cores = []
    for step in range(step_count):
        gotten = lax.psum(
            pick_cores(plan_ids[step], cores, owner_map).astype(jnp.bfloat16), ("owner", "sub")
        )
        step_cores.append(gotten)
    positions = lax.broadcasted_iota(jnp.int32, (segs_n, SEG), 1)
    adapted_list = []
    for step in range(step_count):
        plan_width = step_cores[step].shape[0]
        entries = jnp.arange(plan_width, dtype=jnp.int32)
        selector = (seg_slot[step][:, None] == entries[None, :]).astype(jnp.bfloat16)
        seg_core = jnp.dot(
            selector,
            step_cores[step].reshape(plan_width, rank_full * rank_local),
            preferred_element_type=jnp.float32,
        )
        seg_core = seg_core.astype(jnp.bfloat16).reshape(segs_n, rank_full, rank_local)
        adapted_output = jnp.einsum(
            "sqr,srk->sqk", shrunk[step], seg_core, preferred_element_type=jnp.float32
        )
        alive_mask = positions < seg_length[step][:, None]
        adapted_output = jnp.where(alive_mask[:, :, None], adapted_output, jnp.float32(0.0)).astype(
            jnp.bfloat16
        )
        adapted_list.append(adapted_output.reshape(row_count, rank_local))
    adapted_all = jnp.stack(adapted_list)
    column_slice = out_weight.shape[1]
    frozen_product = jnp.dot(flattened, out_weight, preferred_element_type=jnp.float32)
    adapter_product = jnp.dot(
        adapted_all.reshape(step_count * row_count, rank_local),
        common_expand_matrix,
        preferred_element_type=jnp.float32,
    )
    stacked_results = (frozen_product + adapter_product).reshape(
        step_count, row_count, column_slice
    )
    return lax.psum_scatter(stacked_results, "tensor", scatter_dimension=1, tiled=True).astype(
        jnp.bfloat16
    )


def solution(mesh):
    return jax.shard_map(
        shards,
        mesh=mesh,
        in_specs=(
            P(None, "group", "tensor"),
            P("tensor", ("owner", "sub")),
            P("tensor", None),
            P("tensor", ("owner", "sub")),
            P(("owner", "sub"), None, "tensor"),
            P("group", None),
            P("group", None),
            P("group", None),
            P(),
        ),
        out_specs=P(None, ("group", "tensor"), ("owner", "sub")),
        check_vma=False,
    )
```

profile of v0, /device:TPU:0, one launch (start us, length us, event | category | flops | bytes accessed | tf_op | source)
XLA Modules:
  0.0 737.5 jit_solution(9336982876545404106)
XLA Ops:
  6.5 0.0 copy-start
  6.5 0.0 copy-start.3
  6.5 0.0 all-reduce.4.cloned.1.call-start
  6.5 0.9 fusion.18
  7.4 1.3 gather_fusion
  8.8 1.3 gather_fusion.4
  10.1 1.3 gather_fusion.2
  11.5 4.0 gather_fusion.5
  15.6 0.2 fusion.11
  15.8 1.2 copy.28
  17.0 4.0 gather_fusion.3
  21.0 0.2 fusion.10
  21.2 1.2 copy.29
  22.4 4.0 gather_fusion.1
  26.5 0.2 fusion.9
  26.6 1.2 copy.30
  27.9 0.0 all-reduce.4.cloned.1.call-update
  27.9 0.0 reduce-scatter.2.cloned.1.call-start
  28.0 0.0 copy-done.3
  28.0 0.0 copy-done
  28.0 11.3 %fusion.28 = f32[3072,512]{1,0:T(8,128)} fusion(bf16[3072,2048]{1,0:T(8,128)(2,1)} %bitcast.89, bf16[2048,512]{1,0:T(8,128)(2,1)S(1)} %copy-done), kind=kOutput, calls=%fused_computation.93 | convolution fusion | flops 6442450944 | bytes 20971520 | tf_op jit(solution)/shard_map/dot_general | solution.py:35
  39.3 0.0 copy-start.4
  39.3 217.8 %all-reduce.5 = bf16[3072,512]{1,0:T(8,128)(2,1)} all-reduce(f32[3072,512]{1,0:T(8,128)} %fusion.28), channel_id=1, replica_groups=mesh['group'=2,'tensor'=4,'owner'=2,'sub'=2] {'tensor'}, use_global_device_ids=true, to_apply=%region_0.0 | all-reduce | flops 1572864 | bytes 9437184 | tf_op jit(solution)/shard_map/psum | solution.py:36
  257.1 0.1 iota_compare_fusion.5
  257.2 0.1 iota_compare_fusion.1
  257.3 0.0 copy-done.4
  257.3 3.5 fusion.27
  260.7 0.0 all-reduce.4.cloned.1.call-done
  260.7 0.0 copy-start.2
  260.7 1.6 fusion.2
  262.3 1.5 fusion.1
  263.9 1.5 fusion
  265.4 1.7 fusion.5
  267.1 1.7 fusion.3
  268.8 0.5 fusion.4
  269.3 0.0 slice-start
  269.3 0.1 pad_maximum_fusion
  269.4 0.0 copy-done.2
  269.4 0.0 slice-start.1
  269.4 10.4 %fusion.29 = f32[3072,2048]{1,0:T(8,128)} fusion(bf16[3072,128]{1,0:T(8,128)(2,1)S(1)} %bitcast.79, bf16[128,2048]{1,0:T(8,128)(2,1)S(1)} %copy-done.2), kind=kOutput, calls=%fused_computation.94 | convolution fusion | flops 1610612736 | bytes 26476544 | tf_op jit(solution)/shard_map/dot_general | solution.py:67
  279.8 0.0 slice-done
  279.8 0.0 slice-done.1
  279.8 33.0 %convolution_add_fusion = f32[3072,2048]{1,0:T(8,128)} fusion(f32[3072,2048]{1,0:T(8,128)} %fusion.29, bf16[3072,2048]{1,0:T(8,128)(2,1)} %bitcast.90, bf16[2048,2048]{1,0:T(8,128)(2,1)S(1)} %bitcast.92), kind=kOutput, calls=%fused_computation.9 | convolution fusion | flops 25776095232 | bytes 71303168 | tf_op jit(solution)/shard_map/dot_general | solution.py:66
  312.8 0.0 reduce-scatter.2.cloned.1.call-update
  312.8 0.0 copy-start.1
  312.8 413.0 %reduce-scatter.2.cloned.1.call-done = f32[3,256,2048]{2,1,0:T(8,128)} async-done(((f32[3,1024,2048]{2,1,0:T(8,128)}), f32[3,256,2048]{2,1,0:T(8,128)}) %reduce-scatter.2.cloned.1.call-update) | async-done | bytes 6291472 | tf_op jit(solution)/shard_map/reduce_scatter | solution.py:75
  725.8 4.9 convert_element_type.58
  730.7 0.0 copy-done.1
  (14 shorter events, 0.1 us)
Async XLA Ops:
  6.5 21.4 %copy-start = (bf16[2048,512]{1,0:T(8,128)(2,1)S(1)}, bf16[2048,512]{1,0:T(8,128)(2,1)}, u32[]{:S(2)}) copy-start(bf16[2048,512]{1,0:T(8,128)(2,1)} %param.11) | copy-start | bytes 6291460
  6.5 21.4 %copy-start.3 = (s32[3,8]{1,0:T(4,128)S(1)}, s32[3,8]{1,0:T(4,128)}, u32[]{:S(2)}) copy-start(s32[3,8]{1,0:T(4,128)} %param.16) | copy-start | bytes 292
  6.5 254.2 %all-reduce.4.cloned.1.call-start = ((), (), s32[]{:S(2)}) async-start(), calls=%async_computation.2 | async-start | bytes 3145728 | tf_op jit(solution)/shard_map/psum | solution.py:40
  27.9 697.9 %reduce-scatter.2.cloned.1.call-start = ((), (), s32[]{:S(2)}) async-start(), calls=%async_computation.1 | async-start | bytes 31457280 | tf_op jit(solution)/shard_map/reduce_scatter | solution.py:75
  39.3 217.9 %copy-start.4 = (s32[3,8]{1,0:T(4,128)S(1)}, s32[3,8]{1,0:T(4,128)}, u32[]{:S(2)}) copy-start(s32[3,8]{1,0:T(4,128)} %param.15) | copy-start | bytes 292
  260.7 8.6 %copy-start.2 = (bf16[128,2048]{1,0:T(8,128)(2,1)S(1)}, bf16[128,2048]{1,0:T(8,128)(2,1)}, u32[]{:S(2)}) copy-start(bf16[128,2048]{1,0:T(8,128)(2,1)} %param.12) | copy-start | bytes 1572868
  269.3 10.5 %slice-start = ((s8[8388608]{0:T(1024)(128)(4,1)}), s8[4194304]{0:T(1024)(128)(4,1)S(1)}, s32[]{:S(2)}) async-start(s8[8388608]{0:T(1024)(128)(4,1)} %bitcast.91), calls=%async_computation.3 | async-start | bytes 8388608
  269.4 10.4 %slice-start.1 = ((s8[8388608]{0:T(1024)(128)(4,1)}), s8[4194304]{0:T(1024)(128)(4,1)S(1)}, s32[]{:S(2)}) async-start(s8[8388608]{0:T(1024)(128)(4,1)} %bitcast.91), calls=%async_computation.4 | async-start | bytes 8388608
  312.8 417.9 %copy-start.1 = (bf16[2048,512]{1,0:T(8,128)(2,1)S(1)}, bf16[2048,512]{1,0:T(8,128)(2,1)}, u32[]{:S(2)}) copy-start(bf16[2048,512]{1,0:T(8,128)(2,1)} %param.11) | copy-start | bytes 6291460
Sparse Core Ops, SparseCore 0:
  28.0 45.9 all-reduce.3
  312.9 412.8 reduce-scatter.1
where the time goes:
time: 738 us
  waiting for transfers between devices  413 us (56%)
  blocking collectives  218 us (30%)
  matrix products  63.2 us (9%)
  local copies, waits for them, and re-layouts  23.3 us (3%)
  between operations  13.6 us (2%)
    reduce_scatter x1, waiting for transfers between devices, shards(): lax.psum_scatter(stacked_results, 'tensor', scatter_dimension=1, tiled=True)  413 us
    psum x1, blocking collectives, shards(): shrunk = lax.psum(partial_value, 'tensor').astype(jnp.bfloat16)  218 us
    dot_general x1, matrix products, shards(): jnp.dot(flattened, out_weight, preferred_element_type=jnp.float32)  33 us
  transfers between devices with their start and end apart: 2, of which 1 were waited for; matrix products, arithmetic and copies ran while one was open for 2% of the time, Pallas kernels for 0%

commit v1 on v0

v1 whole, which is shorter than its diff:
```python
import jax
import jax.numpy as jnp
from jax import lax
from jax.sharding import PartitionSpec as P

SEG = 128


def shards(
    activations,
    out_weight,
    shrink_base,
    common_expand_matrix,
    cores,
    plan_ids,
    seg_slot,
    seg_length,
    owner_map,
):
    f32, bf16 = jnp.float32, jnp.bfloat16
    step_count, row_count, feat_local = activations.shape
    segs_n = row_count // SEG
    rank_full = shrink_base.shape[1]
    rank_local = cores.shape[2]
    column_slice = out_weight.shape[1]
    per_device = cores.shape[0]
    plan_width = plan_ids.shape[1]
    spread = lax.axis_size(("owner", "sub"))
    place = lax.axis_index(("owner", "sub"))
    flattened = activations.reshape(step_count * row_count, feat_local)

    share = rank_full // spread
    base_share = lax.dynamic_slice_in_dim(shrink_base, place * share, share, axis=1)
    partial_value = jnp.dot(flattened, base_share, preferred_element_type=f32)
    summed = lax.psum_scatter(partial_value, "tensor", scatter_dimension=0, tiled=True)
    summed = summed.astype(bf16)
    shrunk = lax.all_gather(summed, "tensor", axis=0, tiled=True)
    shrunk = lax.all_gather(shrunk, ("owner", "sub"), axis=1, tiled=True)
    shrunk = shrunk.reshape(step_count, segs_n, SEG, rank_full)

    slots = owner_map[plan_ids.reshape(-1)]
    mine = (slots // per_device) == place
    local_index = slots % per_device
    picked = [
        jnp.where(mine[k], lax.dynamic_index_in_dim(cores, local_index[k], 0, keepdims=False), 0)
        for k in range(step_count * plan_width)
    ]
    plan_cores = lax.psum(jnp.stack(picked), ("owner", "sub"))
    plan_cores = plan_cores.reshape(step_count, plan_width, rank_full, rank_local)

    positions = lax.broadcasted_iota(jnp.int32, (segs_n, SEG), 1)
    results = []
    frozen = [
        jnp.dot(activations[step], out_weight, preferred_element_type=f32)
        for step in range(step_count)
    ]
    for step in range(step_count):
        seg_core = jnp.stack(
            [
                lax.dynamic_index_in_dim(plan_cores[step], seg_slot[step, seg], 0, keepdims=False)
                for seg in range(segs_n)
            ]
        )
        adapted = jnp.einsum("sqr,srk->sqk", shrunk[step], seg_core, preferred_element_type=f32)
        alive = positions < seg_length[step][:, None]
        adapted = jnp.where(alive[:, :, None], adapted, f32(0.0)).astype(bf16)
        adapter_product = jnp.dot(
            adapted.reshape(row_count, rank_local),
            common_expand_matrix,
            preferred_element_type=f32,
        )
        total = (frozen[step] + adapter_product).astype(bf16)
        results.append(lax.psum_scatter(total, "tensor", scatter_dimension=0, tiled=True))
    return jnp.stack(results)


def solution(mesh):
    return jax.shard_map(
        shards,
        mesh=mesh,
        in_specs=(
            P(None, "group", "tensor"),
            P("tensor", ("owner", "sub")),
            P("tensor", None),
            P("tensor", ("owner", "sub")),
            P(("owner", "sub"), None, "tensor"),
            P("group", None),
            P("group", None),
            P("group", None),
            P(),
        ),
        out_specs=P(None, ("group", "tensor"), ("owner", "sub")),
        check_vma=False,
    )
```

time: 738 us -> 402 us (0.54)
  waiting for transfers between devices: 413 us -> 169 us
  blocking collectives: 218 us -> 21.7 us
  between operations: 13.6 us -> 82.2 us
  other arithmetic: 6.67 us -> 23.8 us
  matrix products: 63.2 us -> 78.9 us
    reduce_scatter x1 -> x4, waiting for transfers between devices: 413 us -> 156 us  [the longest x3 156 us: shards(): lax.psum_scatter(total, 'tensor', scatter_dimension=0, tiled=True)]
    psum x1 -> x0, blocking collectives: 218 us -> none  [shards(): shrunk = lax.psum(partial_value, 'tensor').astype(jnp.bfloat16)]
    all_gather x0 -> x1, blocking collectives: none -> 21.7 us  [shards(): shrunk = lax.all_gather(summed, 'tensor', axis=0, tiled=True)]
    unnamed x4 -> x11, other arithmetic: 0.52 us -> 17.2 us
    gather x6 -> x1, local copies, waits for them, and re-layouts: 16 us -> 0.66 us  [shards(): slots = owner_map[plan_ids.reshape(-1)]]
    dot_general x6 -> x7, matrix products: 59.3 us -> 73.7 us  [the longest x3 43.8 us: shards(): jnp.dot(activations[step], out_weight, preferred_element_type=f32)]
    all_gather x0 -> x1, waiting for transfers between devices: none -> 13.7 us  [shards(): shrunk = lax.all_gather(shrunk, ('owner', 'sub'), axis=1, tiled=True)]
  transfers between devices with their start and end apart: 2 -> 6, of which waited for: 1 -> 3; matrix products, arithmetic and copies ran while one was open for 2% -> 23% of each run, Pallas kernels for 0% -> 0%
where the time goes in v1:
time: 402 us; the launch traced here: 400 us
  waiting for transfers between devices  169 us (42%)
  between operations  82.2 us (20%)
  matrix products  78.9 us (20%)
  other arithmetic  23.8 us (6%)
  local copies, waits for them, and re-layouts  23.7 us (6%)
  blocking collectives  21.7 us (5%)
    reduce_scatter x3, waiting for transfers between devices, shards(): lax.psum_scatter(total, 'tensor', scatter_dimension=0, tiled=True)  156 us
    dot_general x3, matrix products, shards(): jnp.dot(activations[step], out_weight, preferred_element_type=f32)  43.8 us
    all_gather x1, blocking collectives, shards(): shrunk = lax.all_gather(summed, 'tensor', axis=0, tiled=True)  21.7 us
    dot_general x3, matrix products, shards(): jnp.dot(adapted.reshape(row_count, rank_local), common_expand_matrix, pre...  19.8 us
    unnamed x11, other arithmetic  17.2 us
    all_gather x1, waiting for transfers between devices, shards(): shrunk = lax.all_gather(shrunk, ('owner', 'sub'), axis=1, tiled=True)  13.7 us
    dot_general x1, matrix products, shards(): partial_value = jnp.dot(flattened, base_share, preferred_element_type=f32)  9.98 us
    unnamed x41, local copies, waits for them, and re-layouts  9.7 us
  transfers between devices with their start and end apart: 6, of which 3 were waited for; matrix products, arithmetic and copies ran while one was open for 23% of the time, Pallas kernels for 0%

profile of v1, /device:TPU:0, one launch (start us, length us, event | category | flops | bytes accessed | tf_op | source)
XLA Modules:
  0.0 400.1 jit_solution(14711219837505353409)
XLA Ops:
  7.4 1.6 copy-done
  9.0 10.0 %convolution_bitcast_fusion = f32[3072,128]{0,1:T(8,128)} fusion(bf16[3072,2048]{1,0:T(8,128)(2,1)} %bitcast.93, bf16[2048,512]{1,0:T(8,128)(2,1)S(1)} %copy-done, s32[]{:T(128)S(6)} %select_n.231), kind=kOutput, calls=%fused_computation.13 | convolution fusion | flops 1610612736 | bytes 14680068 | tf_op jit(solution)/shard_map/dot_general | solution.py:34
  19.0 0.0 all-reduce.2.cloned.1.call-start
  19.1 0.1 reshape.127
  19.2 0.7 gather_fusion
  19.8 0.7 fusion.21
  42.7 0.7 fusion.20
  43.3 1.6 select_dynamic-update-slice_fusion.11
  44.9 1.6 select_dynamic-update-slice_fusion.10
  46.5 1.6 select_dynamic-update-slice_fusion.9
  48.1 1.6 select_dynamic-update-slice_fusion.8
  49.7 1.5 select_dynamic-update-slice_fusion.7
  51.2 1.6 select_dynamic-update-slice_fusion.6
  52.8 1.6 select_dynamic-update-slice_fusion.5
  54.4 1.6 select_dynamic-update-slice_fusion.4
  55.9 1.6 select_dynamic-update-slice_fusion.3
  57.5 1.5 select_dynamic-update-slice_fusion.2
  59.0 1.6 select_dynamic-update-slice_fusion.1
  60.6 1.5 select_dynamic-update-slice_fusion
  62.1 1.1 copy-done.4
  63.2 0.0 all-reduce.2.cloned.1.call-update
  63.3 0.0 all-gather.2.cloned.1.call-start
  63.3 0.0 reduce-scatter.5.cloned.1.call-done
  63.3 1.0 convert_element_type.34
  64.4 21.7 %all_gather.6 = bf16[3072,128]{0,1:T(8,128)(2,1)} all-gather(bf16[768,128]{0,1:T(8,128)(2,1)S(1)} %convert_element_type.34), channel_id=1, replica_groups=mesh['group'=2,'tensor'=4,'owner'=2,'sub'=2] {'tensor'}, dimensions={0}, use_global_device_ids=true | all-gather | bytes 983040 | tf_op jit(solution)/shard_map/all_gather | solution.py:37
  86.1 0.0 all-gather.2.cloned.1.call-update
  86.1 0.0 reduce-scatter.7.cloned.1.call-start
  86.2 0.7 fusion.19
  90.6 0.7 fusion.18
  103.1 0.1 iota_compare_fusion.2
  103.1 14.6 %fusion.4 = f32[1024,2048]{1,0:T(8,128)} fusion(bf16[2048,2048]{1,0:T(8,128)(2,1)} %param.10, bf16[3,1024,2048]{2,1,0:T(8,128)(2,1)} %param.9), kind=kOutput, calls=%fused_computation.8 | convolution fusion | flops 8589934592 | bytes 20971520 | tf_op jit(solution)/shard_map/dot_general | solution.py:54
  117.8 1.8 fusion.17
  119.6 0.7 dynamic-slice_dynamic-update-slice_fusion.23
  120.3 0.7 dynamic-slice_dynamic-update-slice_fusion.22
  120.9 0.7 dynamic-slice_dynamic-update-slice_fusion.21
  121.6 0.7 dynamic-slice_dynamic-update-slice_fusion.20
  122.3 0.7 dynamic-slice_dynamic-update-slice_fusion.19
  122.9 0.7 dynamic-slice_dynamic-update-slice_fusion.18
  123.6 0.7 dynamic-slice_dynamic-update-slice_fusion.17
  124.3 0.7 dynamic-slice_dynamic-update-slice_fusion.16
  124.9 13.7 %all-gather.2.cloned.1.call-done = bf16[3072,512]{0,1:T(8,128)(2,1)} async-done(((bf16[3072,128]{0,1:T(8,128)(2,1)}), bf16[3072,512]{0,1:T(8,128)(2,1)}) %all-gather.2.cloned.1.call-update) | async-done | bytes 3145744 | tf_op jit(solution)/shard_map/all_gather | solution.py:38
  138.6 3.5 fusion.16
  142.2 2.3 copy.16
  144.5 2.0 fusion.9
  146.5 6.6 %add_convert_fusion.2 = bf16[1024,2048]{1,0:T(8,128)(2,1)} fusion(f32[1024,2048]{1,0:T(8,128)} %fusion.4, bf16[1024,128]{1,0:T(8,128)(2,1)S(1)} %bitcast.100, bf16[128,2048]{1,0:T(8,128)(2,1)S(1)} %copy-done.3), kind=kOutput, calls=%fused_computation.3 | convolution fusion | flops 541065216 | bytes 13369344 | tf_op jit(solution)/shard_map/dot_general | solution.py:67
  153.1 0.0 reduce-scatter.7.cloned.1.call-update
  153.1 0.2 reduce-scatter.11.cloned.1.call-start
  183.1 0.1 iota_compare_fusion
  183.2 14.6 %fusion = f32[1024,2048]{1,0:T(8,128)} fusion(bf16[2048,2048]{1,0:T(8,128)(2,1)} %param.10, bf16[3,1024,2048]{2,1,0:T(8,128)(2,1)} %param.9), kind=kOutput, calls=%fused_computation.4 | convolution fusion | flops 8589934592 | bytes 20971520 | tf_op jit(solution)/shard_map/dot_general | solution.py:54
  198.3 1.0 copy-done.6
  199.3 1.0 copy-done.7
  200.2 1.5 copy.18
  201.7 1.6 fusion.11
  203.4 6.7 %add_convert_fusion = bf16[1024,2048]{1,0:T(8,128)(2,1)} fusion(f32[1024,2048]{1,0:T(8,128)} %fusion, bf16[1024,128]{1,0:T(8,128)(2,1)S(1)} %bitcast.101, bf16[128,2048]{1,0:T(8,128)(2,1)S(1)} %copy-done.3), kind=kOutput, calls=%fused_computation.1 | convolution fusion | flops 541065216 | bytes 13369344 | tf_op jit(solution)/shard_map/dot_general | solution.py:67
  210.1 0.0 reduce-scatter.9.cloned.1.call-start
  210.1 14.6 %fusion.2 = f32[1024,2048]{1,0:T(8,128)} fusion(bf16[2048,2048]{1,0:T(8,128)(2,1)} %param.10, bf16[3,1024,2048]{2,1,0:T(8,128)(2,1)} %param.9), kind=kOutput, calls=%fused_computation.6 | convolution fusion | flops 8589934592 | bytes 20971520 | tf_op jit(solution)/shard_map/dot_general | solution.py:54
  224.8 0.5 copy.17
  225.3 1.6 fusion.10
  226.9 6.6 %add_convert_fusion.1 = bf16[1024,2048]{1,0:T(8,128)(2,1)} fusion(f32[1024,2048]{1,0:T(8,128)} %fusion.2, bf16[1024,128]{1,0:T(8,128)(2,1)S(1)} %bitcast.102, bf16[128,2048]{1,0:T(8,128)(2,1)S(1)} %copy-done.3), kind=kOutput, calls=%fused_computation.2 | convolution fusion | flops 541065216 | bytes 13369344 | tf_op jit(solution)/shard_map/dot_general | solution.py:67
  233.5 0.0 reduce-scatter.9.cloned.1.call-update
  233.6 0.0 reduce-scatter.7.cloned.1.call-done
  233.6 76.1 %reduce-scatter.11.cloned.1.call-done = bf16[256,2048]{1,0:T(8,128)(2,1)} async-done(((bf16[1024,2048]{1,0:T(8,128)(2,1)}), bf16[256,2048]{1,0:T(8,128)(2,1)}) %reduce-scatter.11.cloned.1.call-update) | async-done | bytes 1048592 | tf_op jit(solution)/shard_map/reduce_scatter | solution.py:73
  309.7 79.5 %reduce-scatter.9.cloned.1.call-done = bf16[256,2048]{1,0:T(8,128)(2,1)} async-done(((bf16[1024,2048]{1,0:T(8,128)(2,1)}), bf16[256,2048]{1,0:T(8,128)(2,1)}) %reduce-scatter.9.cloned.1.call-update) | async-done | bytes 1048592 | tf_op jit(solution)/shard_map/reduce_scatter | solution.py:73
  389.2 3.9 pad_maximum_fusion
  (40 shorter events, 0.5 us)
Async XLA Ops:
  7.4 1.6 copy-start
  7.4 56.0 %reduce-scatter.5.cloned.1.call-start = ((), (), s32[]{:S(2)}) async-start(), calls=%async_computation.4 | async-start | bytes 1966080 | tf_op jit(solution)/shard_map/reduce_scatter | solution.py:35
  9.0 10.1 %copy-start.8 = (s32[3,4]{1,0:T(4,128)S(1)}, s32[3,4]{1,0:T(4,128)}, u32[]{:S(2)}) copy-start(s32[3,4]{1,0:T(4,128)} %param.14) | copy-start | bytes 148
  9.0 10.2 %copy-start.2 = (s32[256]{0:T(256)S(1)}, s32[256]{0:T(256)}, u32[]{:S(2)}) copy-start(s32[256]{0:T(256)} %param.17) | copy-start | bytes 3076
  19.0 67.2 %copy-start.5 = (s32[3,8]{1,0:T(4,128)S(1)}, s32[3,8]{1,0:T(4,128)}, u32[]{:S(2)}) copy-start(s32[3,8]{1,0:T(4,128)} %param.15) | copy-start | bytes 292
  19.0 84.1 %copy-start.9 = (s32[3,8]{1,0:T(4,128)S(1)}, s32[3,8]{1,0:T(4,128)}, u32[]{:S(2)}) copy-start(s32[3,8]{1,0:T(4,128)} %param.16) | copy-start | bytes 292
  19.0 98.8 %all-reduce.2.cloned.1.call-start = ((), (), s32[]{:S(2)}) async-start(), calls=%async_computation.6 | async-start | bytes 3145728 | tf_op jit(solution)/shard_map/psum | solution.py:48
  62.1 1.1 copy-start.4
  63.3 75.4 %all-gather.2.cloned.1.call-start = ((), (), s32[]{:S(2)}) async-start(), calls=%async_computation.5 | async-start | bytes 3932160 | tf_op jit(solution)/shard_map/all_gather | solution.py:38
  86.1 147.5 %reduce-scatter.7.cloned.1.call-start = ((), (), s32[]{:S(2)}) async-start(), calls=%async_computation.7 | async-start | bytes 5242880 | tf_op jit(solution)/shard_map/reduce_scatter | solution.py:73
  124.9 21.5 %copy-start.3 = (bf16[128,2048]{1,0:T(8,128)(2,1)S(1)}, bf16[128,2048]{1,0:T(8,128)(2,1)}, u32[]{:S(2)}) copy-start(bf16[128,2048]{1,0:T(8,128)(2,1)} %param.12) | copy-start | bytes 1572868
  153.1 156.6 %reduce-scatter.11.cloned.1.call-start = ((), (), s32[]{:S(2)}) async-start(), calls=%async_computation.9 | async-start | bytes 5242880 | tf_op jit(solution)/shard_map/reduce_scatter | solution.py:73
  198.3 1.0 copy-start.6
  199.3 1.0 copy-start.7
  210.1 179.1 %reduce-scatter.9.cloned.1.call-start = ((), (), s32[]{:S(2)}) async-start(), calls=%async_computation.8 | async-start | bytes 5242880 | tf_op jit(solution)/shard_map/reduce_scatter | solution.py:73
  233.6 159.4 %copy-start.1 = (bf16[2048,512]{1,0:T(8,128)(2,1)S(1)}, bf16[2048,512]{1,0:T(8,128)(2,1)}, u32[]{:S(2)}) copy-start(bf16[2048,512]{1,0:T(8,128)(2,1)} %param.11) | copy-start | bytes 6291460
Sparse Core Ops, SparseCore 0:
  19.1 37.9 reduce-scatter.4
  153.2 76.7 reduce-scatter.6
  232.4 77.2 reduce-scatter.10
  311.8 77.2 reduce-scatter.8
Sparse Core Ops, SparseCore 1:
  63.3 45.4 all-reduce.1
  110.2 28.4 all-gather.1

commit v2 on v1

v2 whole, which is shorter than its diff:
```python
import jax
import jax.numpy as jnp
from jax import lax
from jax.sharding import PartitionSpec as P

SEG = 128


def shards(
    activations,
    out_weight,
    shrink_base,
    common_expand_matrix,
    cores,
    plan_ids,
    seg_slot,
    seg_length,
    owner_map,
):
    f32, bf16 = jnp.float32, jnp.bfloat16
    step_count, row_count, feat_local = activations.shape
    segs_n = row_count // SEG
    rank_full = shrink_base.shape[1]
    rank_local = cores.shape[2]
    column_slice = out_weight.shape[1]
    per_device = cores.shape[0]
    plan_width = plan_ids.shape[1]
    spread = lax.axis_size(("owner", "sub"))
    place = lax.axis_index(("owner", "sub"))
    share = rank_full // spread
    base_share = lax.dynamic_slice_in_dim(shrink_base, place * share, share, axis=1)

    def shrink_partial(steps, base):
        return jnp.dot(
            steps.reshape(steps.shape[0] * row_count, feat_local), base, preferred_element_type=f32
        )

    def shrink_finish(partial_value):
        summed = lax.psum_scatter(partial_value, "tensor", scatter_dimension=0, tiled=True)
        pieces = lax.all_gather(summed.astype(bf16), ("tensor", "owner", "sub"), axis=0)
        rows = pieces.shape[1]
        pieces = pieces.reshape(-1, spread, rows, share).transpose(0, 2, 1, 3)
        return pieces.reshape(-1, row_count, rank_full)

    first, rest = activations[:1], activations[1:]
    partial_first = shrink_partial(first, base_share)

    partial_first, wanted = lax.optimization_barrier((partial_first, plan_ids.reshape(-1)))
    slots = owner_map[wanted]
    mine = (slots // per_device) == place
    picked = jnp.where(mine[:, None, None], cores[slots % per_device], bf16(0))
    picked, base_later = lax.optimization_barrier((picked, base_share))
    plan_cores = lax.psum(picked, ("owner", "sub"))
    plan_cores = plan_cores.reshape(step_count, plan_width, rank_full, rank_local)
    shrunk_first = shrink_finish(partial_first)
    shrunk_rest = shrink_finish(shrink_partial(rest, base_later))

    positions = lax.broadcasted_iota(jnp.int32, (segs_n, SEG), 1)

    def adapt(step, shrunk):
        each = jnp.einsum(
            "qr,prk->pqk", shrunk, plan_cores[step], preferred_element_type=f32
        ).reshape(plan_width, segs_n, SEG, rank_local)
        alive = positions < seg_length[step][:, None]
        adapted = jnp.zeros((segs_n, SEG, rank_local), f32)
        for entry in range(plan_width):
            chosen = alive & (seg_slot[step] == entry)[:, None]
            adapted = jnp.where(chosen[:, :, None], each[entry], adapted)
        return adapted.astype(bf16).reshape(row_count, rank_local)

    def scatter(total):
        return lax.psum_scatter(total.astype(bf16), "tensor", scatter_dimension=1, tiled=True)

    def freeze(steps):
        return jnp.einsum("sqf,fc->sqc", steps, out_weight, preferred_element_type=f32)

    def expand(adapted):
        return jnp.einsum("sqk,kc->sqc", adapted, common_expand_matrix, preferred_element_type=f32)

    frozen_first = lax.optimization_barrier(freeze(first))
    out_first = scatter(frozen_first + expand(adapt(0, shrunk_first[0])[None]))
    adapted_rest = jnp.stack([adapt(step, shrunk_rest[step - 1]) for step in range(1, step_count)])
    out_rest = scatter(freeze(rest) + expand(adapted_rest))
    return jnp.concatenate([out_first, out_rest])


def solution(mesh):
    return jax.shard_map(
        shards,
        mesh=mesh,
        in_specs=(
            P(None, "group", "tensor"),
            P("tensor", ("owner", "sub")),
            P("tensor", None),
            P("tensor", ("owner", "sub")),
            P(("owner", "sub"), None, "tensor"),
            P("group", None),
            P("group", None),
            P("group", None),
            P(),
        ),
        out_specs=P(None, ("group", "tensor"), ("owner", "sub")),
        check_vma=False,
    )
```

time: 402 us -> 389 us (0.968)
  waiting for transfers between devices: 169 us -> 257 us
  between operations: 82.2 us -> 15.1 us
  blocking collectives: 21.7 us -> 0 us
  other arithmetic: 23.8 us -> 8.88 us
  local copies, waits for them, and re-layouts: 23.7 us -> 31.7 us
  matrix products: 78.9 us -> 74.6 us
    reduce_scatter x4, waiting for transfers between devices: 156 us -> 226 us  [the longest x2 199 us: scatter(): lax.psum_scatter(total.astype(bf16), 'tensor', scatter_dimension=1, tiled...]
    all_gather x1 -> x0, blocking collectives: 21.7 us -> none  [shards(): shrunk = lax.all_gather(summed, 'tensor', axis=0, tiled=True)]
    unnamed x11 -> x0, other arithmetic: 17.2 us -> none
    all_gather x1 -> x2, waiting for transfers between devices: 13.7 us -> 30 us  [shrink_finish(): lax.all_gather(summed.astype(bf16), ('tensor', 'owner', 'sub'), axis=0)]
    unnamed x41 -> x14, local copies, waits for them, and re-layouts: 9.7 us -> 0.73 us
    gather x1 -> x3, local copies, waits for them, and re-layouts: 0.66 us -> 7.71 us  [the longest x2 7.04 us: shards(): picked = jnp.where(mine[:, None, None], cores[slots % per_device], bf16(0))]
    reshape x1 -> x3, local copies, waits for them, and re-layouts: 0.08 us -> 6.07 us  [the longest x2 5.16 us: shrink_finish(): pieces = pieces.reshape(-1, spread, rows, share).transpose(0, 2, 1, 3)]
    slice x6 -> x4, local copies, waits for them, and re-layouts: 8.19 us -> 13.9 us  [the longest x1 8.28 us: shards(): first, rest = (activations[:1], activations[1:])]
  transfers between devices with their start and end apart: 6 -> 7, of which waited for: 3 -> 5; matrix products, arithmetic and copies ran while one was open for 23% -> 27% of each run, Pallas kernels for 0% -> 0%
where the time goes in v2:
time: 389 us; the launch traced here: 388 us
  waiting for transfers between devices  257 us (66%)
  matrix products  74.6 us (19%)
  local copies, waits for them, and re-layouts  31.7 us (8%)
  between operations  15.1 us (4%)
  other arithmetic  8.88 us (2%)
    reduce_scatter x2, waiting for transfers between devices, scatter(): lax.psum_scatter(total.astype(bf16), 'tensor', scatter_dimension=1, tiled...  199 us
    dot_general x2, matrix products, freeze(): jnp.einsum('sqf,fc->sqc', steps, out_weight, preferred_element_type=f32)  38.9 us
    all_gather x2, waiting for transfers between devices, shrink_finish(): lax.all_gather(summed.astype(bf16), ('tensor', 'owner', 'sub'), axis=0)  30 us
    reduce_scatter x2, waiting for transfers between devices, shrink_finish(): lax.psum_scatter(partial_value, 'tensor', scatter_dimension=0, tiled=True)  27.8 us
    dot_general x2, matrix products, expand(): jnp.einsum('sqk,kc->sqc', adapted, common_expand_matrix, preferred_elemen...  18.1 us
    dot_general x2, matrix products, shrink_partial(): jnp.dot(steps.reshape(steps.shape[0] * row_count, feat_local), base, pref...  11.9 us
    slice x1, local copies, waits for them, and re-layouts, shards(): first, rest = (activations[:1], activations[1:])  8.28 us
  transfers between devices with their start and end apart: 7, of which 5 were waited for; matrix products, arithmetic and copies ran while one was open for 27% of the time, Pallas kernels for 0%

profile of v2, /device:TPU:0, one launch (start us, length us, event | category | flops | bytes accessed | tf_op | source)
XLA Modules:
  0.0 387.9 jit_solution(13327457837120781293)
XLA Ops:
  7.4 0.0 copy-start
  7.4 0.0 reduce-scatter.5.cloned.1.call-start
  7.4 0.9 reshape.569
  8.3 0.7 copy-done
  9.0 0.1 constant_dynamic-slice_fusion
  9.0 4.5 %fusion.8 = f32[1024,128]{0,1:T(8,128)} fusion(bf16[2048,128]{1,0:T(8,128)(2,1)S(1)} %constant_dynamic-slice_fusion, bf16[3,1024,2048]{2,1,0:T(8,128)(2,1)} %param.9), kind=kOutput, calls=%fused_computation.19 | convolution fusion | flops 536870912 | bytes 5242880 | tf_op jit(solution)/shard_map/dot_general | solution.py:34
  13.6 0.0 reduce-scatter.5.cloned.1.call-update
  13.6 0.0 copy-start.2
  13.6 0.0 reduce-scatter.9.cloned.1.call-start
  13.7 8.3 %slice.109 = bf16[2,1024,2048]{2,1,0:T(8,128)(2,1)} slice(bf16[3,1024,2048]{2,1,0:T(8,128)(2,1)} %param.9), slice={[1:3], [0:1024], [0:2048]} | slice | bytes 16777216 | tf_op jit(solution)/shard_map/slice | solution.py:45
  22.0 0.0 copy-done.2
  22.0 0.7 gather_fusion
  22.7 5.3 %gather_fusion.1 = bf16[12,512,128]{2,1,0:T(8,128)(2,1)} fusion(bf16[64,512,128]{2,1,0:T(8,128)(2,1)} %param.13, s32[1024]{0:T(1024)S(1)} %pad_clamp_fusion), kind=kCustom, calls=%fused_computation.1 | custom fusion | bytes 3145776 | tf_op jit(solution)/shard_map/gather | solution.py:51
  28.0 1.7 copy.14
  29.7 1.3 broadcast_select_fusion
  31.1 7.3 %convolution_bitcast_fusion.1 = f32[2048,128]{0,1:T(8,128)} fusion(bf16[2048,128]{1,0:T(8,128)(2,1)S(1)} %constant_dynamic-slice_fusion, bf16[2048,2048]{1,0:T(8,128)(2,1)} %bitcast.109), kind=kOutput, calls=%fused_computation.14 | convolution fusion | flops 1073741824 | bytes 9961472 | tf_op jit(solution)/shard_map/dot_general | solution.py:34
  38.4 0.0 reduce-scatter.9.cloned.1.call-update
  38.4 0.0 all-gather.5.cloned.1.call-start
  38.4 0.0 reduce-scatter.5.cloned.1.call-done
  38.5 1.5 convert_element_type.24
  40.0 0.0 all-gather.5.cloned.1.call-update
  40.0 0.0 all-reduce.2.cloned.1.call-start
  40.1 0.5 all-reduce.2.cloned.1.call-update
  40.6 0.0 all-gather.7.cloned.1.call-start
  40.7 27.8 %reduce-scatter.9.cloned.1.call-done = f32[512,128]{0,1:T(8,128)} async-done(((f32[2048,128]{0,1:T(8,128)}), f32[512,128]{0,1:T(8,128)}) %reduce-scatter.9.cloned.1.call-update) | async-done | bytes 262160 | tf_op jit(solution)/shard_map/reduce_scatter | solution.py:39
  68.5 1.6 convert_element_type.27
  70.1 0.0 all-gather.7.cloned.1.call-update
  70.1 0.0 copy-start.5
  70.1 0.0 copy-start.6
  70.1 0.0 reduce-scatter.7.cloned.1.call-start
  70.2 14.7 %convolution_bitcast_fusion = f32[1,1024,2048]{2,1,0:T(8,128)} fusion(bf16[2048,2048]{1,0:T(8,128)(2,1)} %param.10, bf16[3,1024,2048]{2,1,0:T(8,128)(2,1)} %param.9), kind=kOutput, calls=%fused_computation.7 | convolution fusion | flops 8589934592 | bytes 20971520 | tf_op jit(solution)/shard_map/sqf,fc->sqc/dot_general | solution.py:75
  84.9 0.0 copy-done.5
  84.9 0.0 copy-done.6
  85.0 0.1 fusion.46
  85.1 0.0 copy-start.3
  85.1 23.4 %all-gather.5.cloned.1.call-done = bf16[4096,128]{0,1:T(8,128)(2,1)} async-done(((bf16[256,128]{0,1:T(8,128)(2,1)}), bf16[4096,128]{0,1:T(8,128)(2,1)}) %all-gather.5.cloned.1.call-update) | async-done | bytes 1048592 | tf_op jit(solution)/shard_map/all_gather | solution.py:40
  108.5 1.8 reshape.570
  110.3 1.1 copy.15
  111.5 0.4 reshape.595
  111.9 0.0 all-reduce.2.cloned.1.call-done
  111.9 1.8 convolution_bitcast_fusion.4
  113.7 6.7 %fusion.2 = bf16[1,1024,2048]{2,1,0:T(8,128)(2,1)} fusion(f32[1,1024,2048]{2,1,0:T(8,128)} %convolution_bitcast_fusion, bf16[128,2048]{1,0:T(8,128)(2,1)S(1)} %copy-done.3, bf16[4,1024,128]{1,2,0:T(8,128)(2,1)S(1)} %convolution_bitcast_fusion.4, pred[1024]{0:T(1024)(128)(4,1)S(1)} %get-tuple-element.31, pred[1024]{0:T(1024)(128)(4,1)S(1)} %get-tuple-element.32, ...), kind=kOutput, calls=%fused_computation.6 | convolution fusion | flops 541589504 | bytes 14159872 | tf_op jit(solution)/shard_map/sqk,kc->sqc/dot_general | solution.py:78
  120.4 0.0 reduce-scatter.7.cloned.1.call-update
  120.4 0.2 reduce-scatter.11.cloned.1.call-start
  120.7 0.1 fusion.54
  120.7 24.2 %fusion = f32[2,1024,2048]{2,1,0:T(8,128)} fusion(bf16[3,1024,2048]{2,1,0:T(8,128)(2,1)} %param.9, bf16[2048,2048]{1,0:T(8,128)(2,1)} %param.10), kind=kOutput, calls=%fused_computation.3 | convolution fusion | flops 17179869184 | bytes 37748736 | tf_op jit(solution)/shard_map/sqf,fc->sqc/dot_general | solution.py:75
  144.9 6.6 %all-gather.7.cloned.1.call-done = bf16[8192,128]{0,1:T(8,128)(2,1)} async-done(((bf16[512,128]{0,1:T(8,128)(2,1)}), bf16[8192,128]{0,1:T(8,128)(2,1)}) %all-gather.7.cloned.1.call-update) | async-done | bytes 2097168 | tf_op jit(solution)/shard_map/all_gather | solution.py:40
  151.4 3.3 reshape.573
  154.8 1.7 fusion.63
  156.5 2.8 copy.16
  159.3 1.2 reshape.597
  160.6 1.1 copy.17
  161.7 0.4 reshape.598
  162.1 0.0 copy-start.4
  162.1 2.2 convolution_bitcast_fusion.3
  164.3 0.2 fusion.18
  164.5 1.8 convolution_bitcast_fusion.2
  166.3 0.2 fusion.14
  166.5 11.5 %add_convert_fusion = bf16[2,1024,2048]{2,1,0:T(8,128)(2,1)} fusion(f32[2,1024,2048]{2,1,0:T(8,128)} %fusion, bf16[1,1024,128]{1,2,0:T(8,128)(2,1)S(1)} %fusion.14, bf16[1,1024,128]{1,2,0:T(8,128)(2,1)S(1)} %fusion.18, bf16[128,2048]{1,0:T(8,128)(2,1)S(1)} %copy-done.4), kind=kOutput, calls=%fused_computation.2 | convolution fusion | flops 1082392576 | bytes 26214400 | tf_op jit(solution)/shard_map/sqk,kc->sqc/dot_general | solution.py:78
  178.0 0.0 reduce-scatter.11.cloned.1.call-update
  178.0 0.0 copy-start.1
  178.0 51.4 %reduce-scatter.7.cloned.1.call-done = bf16[1,256,2048]{2,1,0:T(8,128)(2,1)} async-done(((bf16[1,1024,2048]{2,1,0:T(8,128)(2,1)}), bf16[1,256,2048]{2,1,0:T(8,128)(2,1)}) %reduce-scatter.7.cloned.1.call-update) | async-done | bytes 1048592 | tf_op jit(solution)/shard_map/reduce_scatter | solution.py:72
  229.4 147.2 %reduce-scatter.11.cloned.1.call-done = bf16[2,256,2048]{2,1,0:T(8,128)(2,1)} async-done(((bf16[2,1024,2048]{2,1,0:T(8,128)(2,1)}), bf16[2,256,2048]{2,1,0:T(8,128)(2,1)}) %reduce-scatter.11.cloned.1.call-update) | async-done | bytes 2097168 | tf_op jit(solution)/shard_map/reduce_scatter | solution.py:72
  376.7 3.8 pad_maximum_fusion
  (10 shorter events, 0.1 us)
Async XLA Ops:
  7.4 1.6 copy-start
  7.4 31.1 %reduce-scatter.5.cloned.1.call-start = ((), (), s32[]{:S(2)}) async-start(), calls=%async_computation.5 | async-start | bytes 655360 | tf_op jit(solution)/shard_map/reduce_scatter | solution.py:39
  13.6 8.4 %copy-start.2 = (s32[256]{0:T(256)S(1)}, s32[256]{0:T(256)}, u32[]{:S(2)}) copy-start(s32[256]{0:T(256)} %param.17) | copy-start | bytes 3076
  13.6 54.8 %reduce-scatter.9.cloned.1.call-start = ((), (), s32[]{:S(2)}) async-start(), calls=%async_computation.7 | async-start | bytes 1310720 | tf_op jit(solution)/shard_map/reduce_scatter | solution.py:39
  38.4 70.1 %all-gather.5.cloned.1.call-start = ((), (), s32[]{:S(2)}) async-start(), calls=%async_computation.9 | async-start | bytes 1114112 | tf_op jit(solution)/shard_map/all_gather | solution.py:40
  40.0 71.9 %all-reduce.2.cloned.1.call-start = ((), (), s32[]{:S(2)}) async-start(), calls=%async_computation.4 | async-start | bytes 3145728 | tf_op jit(solution)/shard_map/psum | solution.py:53
  40.6 110.8 %all-gather.7.cloned.1.call-start = ((), (), s32[]{:S(2)}) async-start(), calls=%async_computation.10 | async-start | bytes 2228224 | tf_op jit(solution)/shard_map/all_gather | solution.py:40
  70.1 14.8 %copy-start.5 = (s32[3,8]{1,0:T(4,128)S(1)}, s32[3,8]{1,0:T(4,128)}, u32[]{:S(2)}) copy-start(s32[3,8]{1,0:T(4,128)} %param.16) | copy-start | bytes 292
  70.1 14.8 %copy-start.6 = (s32[3,8]{1,0:T(4,128)S(1)}, s32[3,8]{1,0:T(4,128)}, u32[]{:S(2)}) copy-start(s32[3,8]{1,0:T(4,128)} %param.15) | copy-start | bytes 292
  70.1 159.3 %reduce-scatter.7.cloned.1.call-start = ((), (), s32[]{:S(2)}) async-start(), calls=%async_computation.6 | async-start | bytes 5242880 | tf_op jit(solution)/shard_map/reduce_scatter | solution.py:72
  85.1 28.7 %copy-start.3 = (bf16[128,2048]{1,0:T(8,128)(2,1)S(1)}, bf16[128,2048]{1,0:T(8,128)(2,1)}, u32[]{:S(2)}) copy-start(bf16[128,2048]{1,0:T(8,128)(2,1)} %param.12) | copy-start | bytes 1572868
  120.4 256.2 %reduce-scatter.11.cloned.1.call-start = ((), (), s32[]{:S(2)}) async-start(), calls=%async_computation.8 | async-start | bytes 10485760 | tf_op jit(solution)/shard_map/reduce_scatter | solution.py:72
  162.1 4.4 %copy-start.4 = (bf16[128,2048]{1,0:T(8,128)(2,1)S(1)}, bf16[128,2048]{1,0:T(8,128)(2,1)}, u32[]{:S(2)}) copy-start(bf16[128,2048]{1,0:T(8,128)(2,1)} %param.12) | copy-start | bytes 1572868
  178.0 202.5 %copy-start.1 = (bf16[2048,512]{1,0:T(8,128)(2,1)S(1)}, bf16[2048,512]{1,0:T(8,128)(2,1)}, u32[]{:S(2)}) copy-start(bf16[2048,512]{1,0:T(8,128)(2,1)} %param.11) | copy-start | bytes 6291460
Sparse Core Ops, SparseCore 0:
  13.7 24.3 reduce-scatter.4
  40.4 27.9 reduce-scatter.8
  70.9 37.5 all-gather.4
  110.7 40.6 all-gather.6
  153.7 75.6 reduce-scatter.6
  231.6 144.9 reduce-scatter.10
Sparse Core Ops, SparseCore 1:
  43.0 46.2 all-reduce.1

commit v3 on v2

v3 whole, which is shorter than its diff:
```python
import jax
import jax.numpy as jnp
from jax import lax
from jax.experimental.layout import Layout, with_layout_constraint
from jax.sharding import PartitionSpec as P

SEG = 128


def shards(
    activations,
    out_weight,
    shrink_base,
    common_expand_matrix,
    cores,
    plan_ids,
    seg_slot,
    seg_length,
    owner_map,
):
    f32, bf16 = jnp.float32, jnp.bfloat16
    step_count, row_count, feat_local = activations.shape
    segs_n = row_count // SEG
    rank_full = shrink_base.shape[1]
    rank_local = cores.shape[2]
    column_slice = out_weight.shape[1]
    per_device = cores.shape[0]
    plan_width = plan_ids.shape[1]
    spread = lax.axis_size(("owner", "sub"))
    place = lax.axis_index(("owner", "sub"))
    own_segs = segs_n // spread
    own_rows = own_segs * SEG
    own = lax.dynamic_slice_in_dim(activations, place * own_rows, own_rows, axis=1)
    partial_value = jnp.dot(
        own.reshape(step_count * own_rows, feat_local), shrink_base, preferred_element_type=f32
    )

    partial_value, wanted = lax.optimization_barrier((partial_value, plan_ids.reshape(-1)))
    slots = owner_map[wanted]
    mine = (slots // per_device) == place
    picked = jnp.where(mine[:, None, None], cores[slots % per_device], bf16(0))
    picked, weight = lax.optimization_barrier((picked, out_weight))
    plan_cores = lax.psum(picked, ("owner", "sub"))
    plan_cores = plan_cores.reshape(step_count, plan_width, rank_full, rank_local)

    summed = lax.psum_scatter(partial_value, "tensor", scatter_dimension=0, tiled=True)
    shrunk = lax.all_gather(summed.astype(bf16), "tensor", axis=0, tiled=True)
    shrunk = shrunk.reshape(step_count, own_rows, rank_full)
    each = jnp.einsum("sqr,sprk->spqk", shrunk, plan_cores, preferred_element_type=f32)
    each = each.reshape(step_count, plan_width, own_segs, SEG, rank_local)
    own_slot = lax.dynamic_slice_in_dim(seg_slot, place * own_segs, own_segs, axis=1)
    own_length = lax.dynamic_slice_in_dim(seg_length, place * own_segs, own_segs, axis=1)
    positions = lax.broadcasted_iota(jnp.int32, (step_count, own_segs, SEG), 2)
    alive = positions < own_length[:, :, None]
    adapted = jnp.zeros((step_count, own_segs, SEG, rank_local), f32)
    for entry in range(plan_width):
        chosen = alive & (own_slot == entry)[:, :, None]
        adapted = jnp.where(chosen[..., None], each[:, entry], adapted)
    adapted = adapted.astype(bf16).reshape(step_count * own_rows, rank_local)
    adapted = lax.all_gather(adapted, ("owner", "sub"), axis=0)
    adapted = adapted.reshape(spread, step_count, own_rows, rank_local).transpose(1, 0, 2, 3)
    adapted = adapted.reshape(step_count, row_count, rank_local)

    def scatter(total):
        return lax.psum_scatter(total.astype(bf16), "tensor", scatter_dimension=1, tiled=True)

    def freeze(steps):
        rows = steps.reshape(-1, feat_local)
        return jnp.dot(rows, weight, preferred_element_type=f32).reshape(*steps.shape[:2], -1)

    def expand(rows):
        flat = rows.reshape(-1, rank_local)
        flat = jnp.dot(flat, common_expand_matrix, preferred_element_type=f32)
        return flat.reshape(*rows.shape[:2], -1)

    frozen_first = jnp.dot(activations[0], weight, preferred_element_type=f32)
    frozen_first = with_layout_constraint(frozen_first, Layout(major_to_minor=(0, 1)))
    frozen_first = lax.optimization_barrier(frozen_first)
    extra_first = jnp.dot(adapted[0], common_expand_matrix, preferred_element_type=f32)
    total_first = (frozen_first + extra_first).astype(bf16)
    total_first = with_layout_constraint(total_first, Layout(major_to_minor=(0, 1)))
    out_first = lax.psum_scatter(total_first, "tensor", scatter_dimension=0, tiled=True)[None]
    out_rest = scatter(freeze(activations[1:]) + expand(adapted[1:]))
    return jnp.concatenate([out_first, out_rest])


def solution(mesh):
    return jax.shard_map(
        shards,
        mesh=mesh,
        in_specs=(
            P(None, "group", "tensor"),
            P("tensor", ("owner", "sub")),
            P("tensor", None),
            P("tensor", ("owner", "sub")),
            P(("owner", "sub"), None, "tensor"),
            P("group", None),
            P("group", None),
            P("group", None),
            P(),
        ),
        out_specs=P(None, ("group", "tensor"), ("owner", "sub")),
        check_vma=False,
    )
```

time: 389 us -> 324 us (0.83)
  waiting for transfers between devices: 257 us -> 193 us
  blocking collectives: 0 us -> 26.7 us
  matrix products: 74.6 us -> 61.6 us
  local copies, waits for them, and re-layouts: 31.7 us -> 19.7 us
    reduce_scatter x2 -> x1, waiting for transfers between devices: 199 us -> 148 us  [scatter(): lax.psum_scatter(total.astype(bf16), 'tensor', scatter_dimension=1, tiled...]
    all_gather x2 -> x0, waiting for transfers between devices: 30 us -> none  [shrink_finish(): lax.all_gather(summed.astype(bf16), ('tensor', 'owner', 'sub'), axis=0)]
    all_gather x0 -> x2, blocking collectives: none -> 26.7 us  [the longest x1 18 us: shards(): shrunk = lax.all_gather(summed.astype(bf16), 'tensor', axis=0, tiled=True)]
    reduce_scatter x2, waiting for transfers between devices: 27.8 us -> 45.2 us  [the longest x1 31.1 us: shards(): lax.psum_scatter(total_first, 'tensor', scatter_dimension=0, tiled=True)]
    dot_general x9 -> x6, matrix products: 74.6 us -> 61.6 us  [the longest x1 24.2 us: freeze(): jnp.dot(rows, weight, preferred_element_type=f32)]
    slice x4 -> x5, local copies, waits for them, and re-layouts: 13.9 us -> 8.43 us  [the longest x3 8.34 us: shards(): out_rest = scatter(freeze(activations[1:]) + expand(adapted[1:]))]
    reshape x2 -> x1, local copies, waits for them, and re-layouts: 5.16 us -> 0.37 us  [shards(): each = each.reshape(step_count, plan_width, own_segs, SEG, rank_local)]
  transfers between devices with their start and end apart: 7 -> 4, of which waited for: 5 -> 3; matrix products, arithmetic and copies ran while one was open for 27% -> 21% of each run, Pallas kernels for 0% -> 0%
where the time goes in v3:
time: 324 us; the launch traced here: 323 us
  waiting for transfers between devices  193 us (60%)
  matrix products  61.6 us (19%)
  blocking collectives  26.7 us (8%)
  local copies, waits for them, and re-layouts  19.7 us (6%)
  between operations  14.7 us (5%)
  other arithmetic  7.37 us (2%)
    reduce_scatter x1, waiting for transfers between devices, scatter(): lax.psum_scatter(total.astype(bf16), 'tensor', scatter_dimension=1, tiled...  148 us
    reduce_scatter x1, waiting for transfers between devices, shards(): lax.psum_scatter(total_first, 'tensor', scatter_dimension=0, tiled=True)  31.1 us
    dot_general x1, matrix products, freeze(): jnp.dot(rows, weight, preferred_element_type=f32)  24.2 us
    all_gather x1, blocking collectives, shards(): shrunk = lax.all_gather(summed.astype(bf16), 'tensor', axis=0, tiled=True)  18 us
    dot_general x1, matrix products, shards(): frozen_first = jnp.dot(activations[0], weight, preferred_element_type=f32)  14.4 us
    reduce_scatter x1, waiting for transfers between devices, shards(): lax.psum_scatter(partial_value, 'tensor', scatter_dimension=0, tiled=True)  14.1 us
    dot_general x1, matrix products, expand(): flat = jnp.dot(flat, common_expand_matrix, preferred_element_type=f32)  11.4 us
    all_gather x1, blocking collectives, shards(): adapted = lax.all_gather(adapted, ('owner', 'sub'), axis=0)  8.66 us
  transfers between devices with their start and end apart: 4, of which 3 were waited for; matrix products, arithmetic and copies ran while one was open for 21% of the time, Pallas kernels for 0%

profile of v3, /device:TPU:0, one launch (start us, length us, event | category | flops | bytes accessed | tf_op | source)
XLA Modules:
  0.0 323.2 jit_solution(5409300821722129276)
XLA Ops:
  7.4 0.0 copy-start
  7.4 0.0 reduce-scatter.4.cloned.1.call-start
  7.4 0.9 reshape.229
  8.3 2.3 constant_dynamic-slice_fusion.2
  10.6 0.0 copy-done
  10.6 0.0 copy-start.2
  10.6 2.9 fusion.15
  13.5 0.0 reduce-scatter.4.cloned.1.call-update
  13.6 0.0 all-reduce.2.cloned.1.call-start
  13.6 0.0 copy-done.2
  13.6 0.7 gather_fusion
  14.3 5.3 %gather_fusion.1 = bf16[12,512,128]{2,1,0:T(8,128)(2,1)} fusion(bf16[64,512,128]{2,1,0:T(8,128)(2,1)} %param.13, s32[1024]{0:T(1024)S(1)} %pad_clamp_fusion), kind=kCustom, calls=%fused_computation.1 | custom fusion | bytes 3145776 | tf_op jit(solution)/shard_map/gather | solution.py:41
  19.7 1.6 broadcast_select_fusion
  21.3 1.6 copy.17
  22.8 0.0 all-reduce.2.cloned.1.call-update
  22.9 0.0 copy-start.4
  22.9 0.0 copy-start.5
  22.9 0.0 reduce-scatter.6.cloned.1.call-start
  22.9 14.4 %convolution_bitcast_fusion = f32[1024,2048]{1,0:T(8,128)} fusion(bf16[2048,2048]{1,0:T(8,128)(2,1)} %param.10, bf16[3,1024,2048]{2,1,0:T(8,128)(2,1)} %param.9), kind=kOutput, calls=%fused_computation.4 | convolution fusion | flops 8589934592 | bytes 20971520 | tf_op jit(solution)/shard_map/dot_general | solution.py:76
  37.4 0.0 copy-done.4
  37.4 0.1 constant_dynamic-slice_fusion.1
  37.4 0.0 copy-done.5
  37.4 0.1 broadcast_compare_fusion.3
  37.5 0.1 fusion.10
  37.7 14.1 %reduce-scatter.4.cloned.1.call-done = f32[192,512]{1,0:T(8,128)} async-done(((f32[768,512]{1,0:T(8,128)}), f32[192,512]{1,0:T(8,128)}) %reduce-scatter.4.cloned.1.call-update) | async-done | bytes 393232 | tf_op jit(solution)/shard_map/reduce_scatter | solution.py:46
  51.7 1.0 convert_element_type.19
  52.8 18.0 %all_gather.6 = bf16[768,512]{1,0:T(8,128)(2,1)S(1)} all-gather(bf16[192,512]{1,0:T(8,128)(2,1)S(1)} %convert_element_type.19), channel_id=1, replica_groups=mesh['group'=2,'tensor'=4,'owner'=2,'sub'=2] {'tensor'}, dimensions={0}, use_global_device_ids=true | all-gather | bytes 983040 | tf_op jit(solution)/shard_map/all_gather | solution.py:47
  70.8 0.0 all-reduce.2.cloned.1.call-done
  70.8 0.0 copy-start.3
  70.8 2.1 convolution_bitcast_fusion.1
  72.9 0.4 copy.24
  73.3 0.1 fusion.14
  73.3 0.8 fusion.6
  74.1 8.7 %all_gather.7 = bf16[4,768,128]{2,1,0:T(8,128)(2,1)S(1)} all-gather(bf16[1,768,128]{2,1,0:T(8,128)(2,1)S(1)} %fusion.6), channel_id=1, replica_groups=mesh['group'=2,'tensor'=4,'owner'=2,'sub'=2] {'owner','sub'}, dimensions={0}, use_global_device_ids=true | all-gather | bytes 983040 | tf_op jit(solution)/shard_map/all_gather | solution.py:60
  82.8 0.0 copy-done.3
  82.8 6.6 %add_convert_fusion.1 = bf16[1024,2048]{1,0:T(8,128)(2,1)} fusion(f32[1024,2048]{1,0:T(8,128)} %convolution_bitcast_fusion, bf16[1024,128]{1,0:T(8,128)(2,1)S(1)} %bitcast.66, bf16[128,2048]{1,0:T(8,128)(2,1)S(1)} %copy-done.3), kind=kOutput, calls=%fused_computation.3 | convolution fusion | flops 541065216 | bytes 13369344 | tf_op jit(solution)/shard_map/dot_general | solution.py:79
  89.4 0.0 reduce-scatter.6.cloned.1.call-update
  89.4 0.2 reduce-scatter.8.cloned.1.call-start
  89.7 8.3 %slice.32 = bf16[2,1024,2048]{2,1,0:T(8,128)(2,1)} slice(bf16[3,1024,2048]{2,1,0:T(8,128)(2,1)} %param.9), slice={[1:3], [0:1024], [0:2048]} | slice | bytes 16777216 | tf_op jit(solution)/shard_map/slice | solution.py:83
  97.9 24.2 %fusion.16 = f32[2048,2048]{0,1:T(8,128)} fusion(bf16[2048,2048]{1,0:T(8,128)(2,1)} %bitcast.59, bf16[2048,2048]{1,0:T(8,128)(2,1)} %param.10), kind=kOutput, calls=%fused_computation.44 | convolution fusion | flops 17179869184 | bytes 33554432 | tf_op jit(solution)/shard_map/dot_general | solution.py:69
  122.2 11.4 %add_convert_fusion = bf16[2,1024,2048]{2,1,0:T(8,128)(2,1)} fusion(f32[2,1024,2048]{2,1,0:T(8,128)} %bitcast.58, bf16[2,1024,128]{2,1,0:T(8,128)(2,1)S(1)} %bitcast.65, bf16[128,2048]{1,0:T(8,128)(2,1)S(1)} %copy-done.3), kind=kOutput, calls=%fused_computation.2 | convolution fusion | flops 1082130432 | bytes 26214400 | tf_op jit(solution)/shard_map/dot_general | solution.py:73
  133.6 0.0 reduce-scatter.8.cloned.1.call-update
  133.6 0.0 copy-start.1
  133.7 31.1 %reduce-scatter.6.cloned.1.call-done = bf16[256,2048]{1,0:T(8,128)(2,1)} async-done(((bf16[1024,2048]{1,0:T(8,128)(2,1)}), bf16[256,2048]{1,0:T(8,128)(2,1)}) %reduce-scatter.6.cloned.1.call-update) | async-done | bytes 1048592 | tf_op jit(solution)/shard_map/reduce_scatter | solution.py:82
  164.8 147.5 %reduce-scatter.8.cloned.1.call-done = bf16[2,256,2048]{2,1,0:T(8,128)(2,1)} async-done(((bf16[2,1024,2048]{2,1,0:T(8,128)(2,1)}), bf16[2,256,2048]{2,1,0:T(8,128)(2,1)}) %reduce-scatter.8.cloned.1.call-update) | async-done | bytes 2097168 | tf_op jit(solution)/shard_map/reduce_scatter | solution.py:65
  312.3 3.8 %pad_maximum_fusion = bf16[3,256,2048]{2,1,0:T(8,128)(2,1)} fusion(bf16[2,256,2048]{2,1,0:T(8,128)(2,1)} %reduce-scatter.8.cloned.1.call-done, bf16[1,256,2048]{2,1,0:T(8,128)(2,1)} %bitcast.67), kind=kLoop, calls=%fused_computation.7 | loop fusion | flops 1572864 | bytes 6291456 | tf_op jit(solution)/shard_map/concatenate | solution.py:84
  316.1 0.0 copy-done.1
  (12 shorter events, 0.2 us)
Async XLA Ops:
  7.4 3.2 copy-start
  7.4 44.4 %reduce-scatter.4.cloned.1.call-start = ((), (), s32[]{:S(2)}) async-start(), calls=%async_computation.4 | async-start | bytes 1966080 | tf_op jit(solution)/shard_map/reduce_scatter | solution.py:46
  10.6 3.0 copy-start.2
  13.6 57.3 %all-reduce.2.cloned.1.call-start = ((), (), s32[]{:S(2)}) async-start(), calls=%async_computation.3 | async-start | bytes 3145728 | tf_op jit(solution)/shard_map/psum | solution.py:43
  22.9 14.5 %copy-start.4 = (s32[3,8]{1,0:T(4,128)S(1)}, s32[3,8]{1,0:T(4,128)}, u32[]{:S(2)}) copy-start(s32[3,8]{1,0:T(4,128)} %param.16) | copy-start | bytes 292
  22.9 14.6 %copy-start.5 = (s32[3,8]{1,0:T(4,128)S(1)}, s32[3,8]{1,0:T(4,128)}, u32[]{:S(2)}) copy-start(s32[3,8]{1,0:T(4,128)} %param.15) | copy-start | bytes 292
  22.9 141.9 %reduce-scatter.6.cloned.1.call-start = ((), (), s32[]{:S(2)}) async-start(), calls=%async_computation.5 | async-start | bytes 5242880 | tf_op jit(solution)/shard_map/reduce_scatter | solution.py:82
  70.8 12.0 %copy-start.3 = (bf16[128,2048]{1,0:T(8,128)(2,1)S(1)}, bf16[128,2048]{1,0:T(8,128)(2,1)}, u32[]{:S(2)}) copy-start(bf16[128,2048]{1,0:T(8,128)(2,1)} %param.12) | copy-start | bytes 1572868
  89.4 222.8 %reduce-scatter.8.cloned.1.call-start = ((), (), s32[]{:S(2)}) async-start(), calls=%async_computation.6 | async-start | bytes 10485760 | tf_op jit(solution)/shard_map/reduce_scatter | solution.py:65
  133.6 182.4 %copy-start.1 = (bf16[2048,512]{1,0:T(8,128)(2,1)S(1)}, bf16[2048,512]{1,0:T(8,128)(2,1)}, u32[]{:S(2)}) copy-start(bf16[2048,512]{1,0:T(8,128)(2,1)} %param.11) | copy-start | bytes 6291460
Sparse Core Ops, SparseCore 0:
  13.7 38.0 reduce-scatter.3
  89.6 75.1 reduce-scatter.5
  167.2 144.9 reduce-scatter.7
Sparse Core Ops, SparseCore 1:
  22.9 45.4 all-reduce.1

commit v4 on v3

--- a/solution.py
+++ b/solution.py
@@ -56,10 +56,13 @@
     for entry in range(plan_width):
         chosen = alive & (own_slot == entry)[:, :, None]
         adapted = jnp.where(chosen[..., None], each[:, entry], adapted)
-    adapted = adapted.astype(bf16).reshape(step_count * own_rows, rank_local)
-    adapted = lax.all_gather(adapted, ("owner", "sub"), axis=0)
-    adapted = adapted.reshape(spread, step_count, own_rows, rank_local).transpose(1, 0, 2, 3)
-    adapted = adapted.reshape(step_count, row_count, rank_local)
+    adapted = adapted.astype(bf16).reshape(step_count, own_rows, rank_local)
+
+    def gather(part):
+        everyones = lax.all_gather(part, ("owner", "sub"), axis=0)
+        return everyones.transpose(1, 0, 2, 3).reshape(part.shape[0], row_count, rank_local)
+
+    adapted_first, adapted_rest = gather(adapted[:1]), adapted[1:]
 
     def scatter(total):
         return lax.psum_scatter(total.astype(bf16), "tensor", scatter_dimension=1, tiled=True)
@@ -76,11 +79,12 @@
     frozen_first = jnp.dot(activations[0], weight, preferred_element_type=f32)
     frozen_first = with_layout_constraint(frozen_first, Layout(major_to_minor=(0, 1)))
     frozen_first = lax.optimization_barrier(frozen_first)
-    extra_first = jnp.dot(adapted[0], common_expand_matrix, preferred_element_type=f32)
+    extra_first = jnp.dot(adapted_first[0], common_expand_matrix, preferred_element_type=f32)
     total_first = (frozen_first + extra_first).astype(bf16)
     total_first = with_layout_constraint(total_first, Layout(major_to_minor=(0, 1)))
     out_first = lax.psum_scatter(total_first, "tensor", scatter_dimension=0, tiled=True)[None]
-    out_rest = scatter(freeze(activations[1:]) + expand(adapted[1:]))
+    _, adapted_rest = lax.optimization_barrier((total_first, adapted_rest))
+    out_rest = scatter(freeze(activations[1:]) + expand(gather(adapted_rest)))
     return jnp.concatenate([out_first, out_rest])
 
 

time: 324 us -> 321 us (level)
  waiting for transfers between devices: 193 us -> 186 us
  blocking collectives: 26.7 us -> 31.2 us
    reduce_scatter x1, waiting for transfers between devices: 31.1 us -> 24.6 us  [shards(): lax.psum_scatter(total_first, 'tensor', scatter_dimension=0, tiled=True)]
    all_gather x1 -> x2, blocking collectives: 8.66 us -> 13.1 us  [gather(): everyones = lax.all_gather(part, ('owner', 'sub'), axis=0)]
  transfers between devices with their start and end apart: 4 -> 4, of which waited for: 3 -> 3; matrix products, arithmetic and copies ran while one was open for 21% -> 22% of each run, Pallas kernels for 0% -> 0%
where the time goes in v4:
time: 321 us
  waiting for transfers between devices  186 us (58%)
  matrix products  61.6 us (19%)
  blocking collectives  31.2 us (10%)
  local copies, waits for them, and re-layouts  19.8 us (6%)
  between operations  14.7 us (5%)
  other arithmetic  7.07 us (2%)
    reduce_scatter x1, waiting for transfers between devices, scatter(): lax.psum_scatter(total.astype(bf16), 'tensor', scatter_dimension=1, tiled...  148 us
    reduce_scatter x1, waiting for transfers between devices, shards(): lax.psum_scatter(total_first, 'tensor', scatter_dimension=0, tiled=True)  24.6 us
    dot_general x1, matrix products, freeze(): jnp.dot(rows, weight, preferred_element_type=f32)  24.2 us
    all_gather x1, blocking collectives, shards(): shrunk = lax.all_gather(summed.astype(bf16), 'tensor', axis=0, tiled=True)  18 us
    dot_general x1, matrix products, shards(): frozen_first = jnp.dot(activations[0], weight, preferred_element_type=f32)  14.5 us
    reduce_scatter x1, waiting for transfers between devices, shards(): lax.psum_scatter(partial_value, 'tensor', scatter_dimension=0, tiled=True)  14 us
    all_gather x2, blocking collectives, gather(): everyones = lax.all_gather(part, ('owner', 'sub'), axis=0)  13.1 us
    dot_general x1, matrix products, expand(): flat = jnp.dot(flat, common_expand_matrix, preferred_element_type=f32)  11.3 us
  transfers between devices with their start and end apart: 4, of which 3 were waited for; matrix products, arithmetic and copies ran while one was open for 22% of the time, Pallas kernels for 0%

profile of v4, /device:TPU:0, one launch (start us, length us, event | category | flops | bytes accessed | tf_op | source)
XLA Modules:
  0.0 320.8 jit_solution(7459351604824083087)
XLA Ops:
  7.4 0.0 copy-start
  7.4 0.0 reduce-scatter.4.cloned.1.call-start
  7.4 0.9 reshape.112
  8.3 2.3 constant_dynamic-slice_fusion.2
  10.6 0.0 copy-done
  10.6 0.0 copy-start.2
  10.6 2.9 fusion.15
  13.5 0.0 reduce-scatter.4.cloned.1.call-update
  13.6 0.0 all-reduce.2.cloned.1.call-start
  13.6 0.0 copy-done.2
  13.6 0.7 gather_fusion
  14.3 5.3 %gather_fusion.1 = bf16[12,512,128]{2,1,0:T(8,128)(2,1)} fusion(bf16[64,512,128]{2,1,0:T(8,128)(2,1)} %param.13, s32[1024]{0:T(1024)S(1)} %pad_clamp_fusion), kind=kCustom, calls=%fused_computation.1 | custom fusion | bytes 3145776 | tf_op jit(solution)/shard_map/gather | solution.py:41
  19.7 1.6 broadcast_select_fusion
  21.3 1.6 copy.21
  22.8 0.0 all-reduce.2.cloned.1.call-update
  22.9 0.0 copy-start.4
  22.9 0.0 copy-start.5
  22.9 0.0 reduce-scatter.6.cloned.1.call-start
  22.9 14.5 %convolution_bitcast_fusion = f32[1024,2048]{1,0:T(8,128)} fusion(bf16[2048,2048]{1,0:T(8,128)(2,1)} %param.10, bf16[3,1024,2048]{2,1,0:T(8,128)(2,1)} %param.9), kind=kOutput, calls=%fused_computation.4 | convolution fusion | flops 8589934592 | bytes 20971520 | tf_op jit(solution)/shard_map/dot_general | solution.py:79
  37.5 0.0 copy-start.3
  37.5 0.0 copy-done.4
  37.5 0.1 constant_dynamic-slice_fusion.1
  37.5 0.0 copy-done.5
  37.6 0.1 broadcast_compare_fusion.3
  37.6 0.1 fusion.11
  37.7 14.0 %reduce-scatter.4.cloned.1.call-done = f32[192,512]{1,0:T(8,128)} async-done(((f32[768,512]{1,0:T(8,128)}), f32[192,512]{1,0:T(8,128)}) %reduce-scatter.4.cloned.1.call-update) | async-done | bytes 393232 | tf_op jit(solution)/shard_map/reduce_scatter | solution.py:46
  51.7 1.0 convert_element_type.12
  52.8 18.0 %all_gather.15 = bf16[768,512]{1,0:T(8,128)(2,1)S(1)} all-gather(bf16[192,512]{1,0:T(8,128)(2,1)S(1)} %convert_element_type.12), channel_id=1, replica_groups=mesh['group'=2,'tensor'=4,'owner'=2,'sub'=2] {'tensor'}, dimensions={0}, use_global_device_ids=true | all-gather | bytes 983040 | tf_op jit(solution)/shard_map/all_gather | solution.py:47
  70.8 0.0 all-reduce.2.cloned.1.call-done
  70.8 2.0 convolution_bitcast_fusion.1
  72.8 0.2 reshape.115
  73.0 0.5 fusion.7
  73.6 0.1 copy.25
  73.7 5.8 %all_gather.17 = bf16[4,1,256,128]{3,2,1,0:T(8,128)(2,1)S(1)} all-gather(bf16[1,1,256,128]{3,2,1,0:T(8,128)(2,1)S(1)} %bitcast.93), channel_id=1, replica_groups=mesh['group'=2,'tensor'=4,'owner'=2,'sub'=2] {'owner','sub'}, dimensions={0}, use_global_device_ids=true | all-gather | bytes 327680 | tf_op jit(solution)/shard_map/all_gather | solution.py:62
  79.5 0.0 copy-done.3
  79.5 6.6 %add_convert_fusion.1 = bf16[1024,2048]{1,0:T(8,128)(2,1)} fusion(f32[1024,2048]{1,0:T(8,128)} %convolution_bitcast_fusion, bf16[1024,128]{1,0:T(8,128)(2,1)S(1)} %bitcast.89, bf16[128,2048]{1,0:T(8,128)(2,1)S(1)} %copy-done.3), kind=kOutput, calls=%fused_computation.3 | convolution fusion | flops 541065216 | bytes 13369344 | tf_op jit(solution)/shard_map/dot_general | solution.py:82
  86.1 0.0 reduce-scatter.6.cloned.1.call-update
  86.1 0.2 reduce-scatter.8.cloned.1.call-start
  86.3 8.3 %slice.34 = bf16[2,1024,2048]{2,1,0:T(8,128)(2,1)} slice(bf16[3,1024,2048]{2,1,0:T(8,128)(2,1)} %param.9), slice={[1:3], [0:1024], [0:2048]} | slice | bytes 16777216 | tf_op jit(solution)/shard_map/slice | solution.py:87
  94.6 24.2 %fusion.16 = f32[2048,2048]{0,1:T(8,128)} fusion(bf16[2048,2048]{1,0:T(8,128)(2,1)} %bitcast.84, bf16[2048,2048]{1,0:T(8,128)(2,1)} %param.10), kind=kOutput, calls=%fused_computation.47 | convolution fusion | flops 17179869184 | bytes 33554432 | tf_op jit(solution)/shard_map/dot_general | solution.py:72
  118.8 0.1 slice.46
  118.9 0.1 copy.26
  119.1 7.3 %all-gather = bf16[8,256,128]{2,1,0:T(8,128)(2,1)S(1)} all-gather(bf16[2,256,128]{2,1,0:T(8,128)(2,1)S(1)} %bitcast.92), channel_id=2, replica_groups=mesh['group'=2,'tensor'=4,'owner'=2,'sub'=2] {'owner','sub'}, dimensions={0}, use_global_device_ids=true | all-gather | bytes 655360 | tf_op jit(solution)/shard_map/all_gather | solution.py:62
  126.4 11.3 %add_convert_fusion = bf16[2,1024,2048]{2,1,0:T(8,128)(2,1)} fusion(f32[2,1024,2048]{2,1,0:T(8,128)} %bitcast.83, bf16[2,1024,128]{2,1,0:T(8,128)(2,1)S(1)} %bitcast.87, bf16[128,2048]{1,0:T(8,128)(2,1)S(1)} %copy-done.3), kind=kOutput, calls=%fused_computation.2 | convolution fusion | flops 1082130432 | bytes 26214400 | tf_op jit(solution)/shard_map/dot_general | solution.py:76
  137.7 0.0 reduce-scatter.8.cloned.1.call-update
  137.8 0.0 copy-start.1
  137.8 24.6 %reduce-scatter.6.cloned.1.call-done = bf16[256,2048]{1,0:T(8,128)(2,1)} async-done(((bf16[1024,2048]{1,0:T(8,128)(2,1)}), bf16[256,2048]{1,0:T(8,128)(2,1)}) %reduce-scatter.6.cloned.1.call-update) | async-done | bytes 1048592 | tf_op jit(solution)/shard_map/reduce_scatter | solution.py:85
  162.4 147.5 %reduce-scatter.8.cloned.1.call-done = bf16[2,256,2048]{2,1,0:T(8,128)(2,1)} async-done(((bf16[2,1024,2048]{2,1,0:T(8,128)(2,1)}), bf16[2,256,2048]{2,1,0:T(8,128)(2,1)}) %reduce-scatter.8.cloned.1.call-update) | async-done | bytes 2097168 | tf_op jit(solution)/shard_map/reduce_scatter | solution.py:68
  309.9 3.8 %pad_maximum_fusion = bf16[3,256,2048]{2,1,0:T(8,128)(2,1)} fusion(bf16[2,256,2048]{2,1,0:T(8,128)(2,1)} %reduce-scatter.8.cloned.1.call-done, bf16[1,256,2048]{2,1,0:T(8,128)(2,1)} %bitcast.90), kind=kLoop, calls=%fused_computation.7 | loop fusion | flops 1572864 | bytes 6291456 | tf_op jit(solution)/shard_map/concatenate | solution.py:88
  313.7 0.0 copy-done.1
  (7 shorter events, 0.1 us)
Async XLA Ops:
  7.4 3.2 %copy-start = (bf16[2048,512]{1,0:T(8,128)(2,1)S(1)}, bf16[2048,512]{1,0:T(8,128)(2,1)}, u32[]{:S(2)}) copy-start(bf16[2048,512]{1,0:T(8,128)(2,1)} %param.11) | copy-start | bytes 6291460
  7.4 44.4 %reduce-scatter.4.cloned.1.call-start = ((), (), s32[]{:S(2)}) async-start(), calls=%async_computation.4 | async-start | bytes 1966080 | tf_op jit(solution)/shard_map/reduce_scatter | solution.py:46
  10.6 3.0 copy-start.2
  13.6 57.3 %all-reduce.2.cloned.1.call-start = ((), (), s32[]{:S(2)}) async-start(), calls=%async_computation.3 | async-start | bytes 3145728 | tf_op jit(solution)/shard_map/psum | solution.py:43
  22.9 14.6 %copy-start.4 = (s32[3,8]{1,0:T(4,128)S(1)}, s32[3,8]{1,0:T(4,128)}, u32[]{:S(2)}) copy-start(s32[3,8]{1,0:T(4,128)} %param.16) | copy-start | bytes 292
  22.9 14.7 %copy-start.5 = (s32[3,8]{1,0:T(4,128)S(1)}, s32[3,8]{1,0:T(4,128)}, u32[]{:S(2)}) copy-start(s32[3,8]{1,0:T(4,128)} %param.15) | copy-start | bytes 292
  22.9 139.5 %reduce-scatter.6.cloned.1.call-start = ((), (), s32[]{:S(2)}) async-start(), calls=%async_computation.5 | async-start | bytes 5242880 | tf_op jit(solution)/shard_map/reduce_scatter | solution.py:85
  37.5 42.0 %copy-start.3 = (bf16[128,2048]{1,0:T(8,128)(2,1)S(1)}, bf16[128,2048]{1,0:T(8,128)(2,1)}, u32[]{:S(2)}) copy-start(bf16[128,2048]{1,0:T(8,128)(2,1)} %param.12) | copy-start | bytes 1572868
  86.1 223.8 %reduce-scatter.8.cloned.1.call-start = ((), (), s32[]{:S(2)}) async-start(), calls=%async_computation.6 | async-start | bytes 10485760 | tf_op jit(solution)/shard_map/reduce_scatter | solution.py:68
  137.8 175.9 %copy-start.1 = (bf16[2048,512]{1,0:T(8,128)(2,1)S(1)}, bf16[2048,512]{1,0:T(8,128)(2,1)}, u32[]{:S(2)}) copy-start(bf16[2048,512]{1,0:T(8,128)(2,1)} %param.11) | copy-start | bytes 6291460
Sparse Core Ops, SparseCore 0:
  13.7 38.0 reduce-scatter.3
  86.2 76.1 reduce-scatter.5
  164.9 144.9 reduce-scatter.7
Sparse Core Ops, SparseCore 1:
  22.9 45.4 all-reduce.1
